TPU v7x, 256 devices: a whole 4x4x8 slice. The times are simulated.
256 devices in a mesh: dp: 16 (over x, y_hi, core), seq: 16 (over z, y_lo).
Axes of the slice: x: 4, y: 4 (y_hi: 2, y_lo: 2; y = y_hi * 2 + y_lo), z: 8, core: 2. Of those that a mesh axis runs over, the one named last changes fastest.
Arguments:
- coarse: bfloat16 [16, 4096, 1024], P('dp', 'seq'), may hold values from -6 to 6
- skip: bfloat16 [16, 8192, 768], P('dp', 'seq'), may hold values from -6 to 6
- conv_weight: bfloat16 [5, 1024, 768], replicated, may hold values from -0.078125 to 0.078125
- donor_weight: bfloat16 [768, 768], replicated, may hold values from -0.21875 to 0.21875
- acceptor_weight: bfloat16 [768, 768], replicated, may hold values from -0.21875 to 0.21875
- other_grad: bfloat16 [16, 8192, 768], P('dp', 'seq'), may hold values from -4 to 4
- score_grad: float32 [16, 1024], P('dp', 'seq'), may hold values from -16 to 16
- donor_pos: int32 [16, 1024], P('dp', 'seq'), may hold values from 0 to 511
- acceptor_pos: int32 [16, 1024], P('dp', 'seq'), may hold values from 0 to 8191, as said below
- pair_mask: int32 [16, 1024], P('dp', 'seq'), may hold values 0 or 1
Outputs:
- scores: float32 [16, 1024], P('dp', 'seq')
- coarse_grad: bfloat16 [16, 4096, 1024], P('dp', 'seq')
- donor_weight_grad: float32 [768, 768], P('seq')
- acceptor_weight_grad: float32 [768, 768], P('seq')
Inputs may be any that keep to these rules, and one draw needn't show every extreme that they name: Position in the whole sample. Among the 64 slots held by one shard of a sample, at most 8 have their acceptor on any one shard (shard = acceptor_pos // 512); in every sample some shard is named by exactly 8 slots of every shard.
All inputs are finite; a program needn't handle non-finite values. No bound on the sum of `pair_mask` on one device may be relied on, other than what follows from the above.
Results may differ from a plain program's by a relative error of at most 0.013.
Values may be sent and summed in bfloat16 or wider, within the bound.
A program may use at most 128 MiB of HBM per device.

v0:
```python
import math
import jax
import jax.numpy as jnp
from jax import lax
from jax.sharding import PartitionSpec as P

ACAP = 8


def with_halo(cells, sides, width):
    for axis, dim in sides:
        count = lax.axis_size(axis)
        ends = count - 1
        head = lax.slice_in_dim(cells, 0, width, axis=dim)
        tail = lax.slice_in_dim(cells, cells.shape[dim] - width, cells.shape[dim], axis=dim)
        cells = jnp.concatenate(
            [
                lax.ppermute(tail, axis, [(i, (i + 1) % count) for i in range(ends)]),
                cells,
                lax.ppermute(head, axis, [((i + 1) % count, i) for i in range(ends)]),
            ],
            axis=dim,
        )
    return cells


def activate(values):
    return jax.nn.gelu(values, approximate=True)


def on_device(
    coarse,
    skip,
    conv_weight,
    donor_weight,
    acceptor_weight,
    other_grad,
    score_grad,
    donor_pos,
    acceptor_pos,
    pair_mask,
):
    seq_count = lax.axis_size("seq")
    batch_count = lax.axis_size("dp")
    taps = conv_weight.shape[0]
    emb_width = donor_weight.shape[1]
    inverse_root = 1.0 / math.sqrt(emb_width)
    widened = with_halo(coarse, (("seq", 1),), 1)
    upsampled = jnp.repeat(widened[0], 2, axis=0)
    row_count = upsampled.shape[0] - 4
    preact = skip[0].astype(jnp.float32)
    for shift_index in range(taps):
        preact = preact + jnp.dot(
            upsampled[shift_index : shift_index + row_count],
            conv_weight[shift_index],
            preferred_element_type=jnp.float32,
        )
    activated = activate(preact).astype(jnp.bfloat16)
    donor_rows = donor_pos[0]
    donor_act = activated[donor_rows]
    donor_emb = jnp.dot(donor_act, donor_weight, preferred_element_type=jnp.float32).astype(
        jnp.bfloat16
    )
    targets = acceptor_pos[0]
    owner = targets // row_count
    local_row = targets % row_count
    owner_hits = (owner[:, None] == jnp.arange(seq_count, dtype=jnp.int32)[None, :]).astype(
        jnp.int32
    )
    place_rank = jnp.sum((jnp.cumsum(owner_hits, axis=0) - owner_hits) * owner_hits, axis=1)
    capacity = ACAP
    slot_index = owner * capacity + place_rank
    requests = (
        jnp.zeros((seq_count * capacity,), jnp.int32)
        .at[slot_index]
        .set(local_row)
        .reshape(seq_count, capacity)
    )
    received = lax.all_to_all(requests, "seq", split_axis=0, concat_axis=0, tiled=True)
    wanted = activated[received.reshape(-1)]
    projected = jnp.dot(wanted, acceptor_weight, preferred_element_type=jnp.float32).astype(
        jnp.bfloat16
    )
    projected = projected.reshape(received.shape[0], received.shape[1], emb_width)
    returned = lax.all_to_all(projected, "seq", split_axis=0, concat_axis=0, tiled=True)
    returned, served_rows = (returned, received)
    acceptor_emb = returned.reshape(seq_count * capacity, emb_width)[slot_index]
    mask_float = pair_mask[0].astype(jnp.float32)
    scores = (
        mask_float
        * jnp.sum(donor_emb.astype(jnp.float32) * acceptor_emb.astype(jnp.float32), axis=1)
        * inverse_root
    )
    weighted = score_grad[0] * mask_float
    donor_emb_grad = (weighted[:, None] * acceptor_emb.astype(jnp.float32) * inverse_root).astype(
        jnp.bfloat16
    )
    acceptor_emb_grad = (weighted[:, None] * donor_emb.astype(jnp.float32) * inverse_root).astype(
        jnp.bfloat16
    )
    outgoing = (
        jnp.zeros((seq_count * capacity, emb_width), jnp.bfloat16)
        .at[slot_index]
        .set(acceptor_emb_grad)
    )
    outgoing = outgoing.reshape(seq_count, capacity, emb_width)
    received = lax.all_to_all(outgoing, "seq", split_axis=0, concat_axis=0, tiled=True)
    flattened = received.reshape(-1, emb_width)
    to_rows = jnp.dot(flattened, acceptor_weight.T, preferred_element_type=jnp.float32)
    row_terms = to_rows.reshape(received.shape[0], received.shape[1], -1)
    served_flat = served_rows.reshape(-1)
    act_grad = other_grad[0].astype(jnp.float32)
    act_grad = act_grad.at[donor_rows].add(
        jnp.dot(donor_emb_grad, donor_weight.T, preferred_element_type=jnp.float32)
    )
    act_grad = act_grad.at[served_flat].add(row_terms.reshape(-1, row_terms.shape[2]))
    pull = jax.vjp(activate, preact)[1]
    preact_grad = pull(act_grad)[0].astype(jnp.bfloat16)
    widened_grad = with_halo(preact_grad[None], (("seq", 1),), 2)[0]
    upsampled_grad = jnp.zeros((row_count, conv_weight.shape[1]), jnp.float32)
    for shift_index in range(taps):
        begin = 4 - shift_index
        upsampled_grad = upsampled_grad + jnp.dot(
            widened_grad[begin : begin + row_count],
            conv_weight[shift_index].T,
            preferred_element_type=jnp.float32,
        )
    coarse_grad = (
        upsampled_grad.reshape(row_count // 2, 2, -1).sum(axis=1).astype(jnp.bfloat16)[None]
    )
    served_act = activated[served_flat]
    served_emb_grad = received.reshape(-1, emb_width)
    rows_each = donor_weight.shape[0] // seq_count
    factor = 1.0 / batch_count
    donor_term = jnp.dot(donor_act.T, donor_emb_grad, preferred_element_type=jnp.float32)
    acceptor_term = jnp.dot(served_act.T, served_emb_grad, preferred_element_type=jnp.float32)
    donor_total, acceptor_total = lax.psum((donor_term, acceptor_term), ("dp", "seq"))
    first_row = lax.axis_index("seq") * rows_each
    donor_part = lax.dynamic_slice_in_dim(donor_total, first_row, rows_each, 0)
    acceptor_part = lax.dynamic_slice_in_dim(acceptor_total, first_row, rows_each, 0)
    return (scores[None], coarse_grad, donor_part * factor, acceptor_part * factor)


def solution(mesh):
    in_specs = (
        P("dp", "seq", None),
        P("dp", "seq", None),
        P(),
        P(),
        P(),
        P("dp", "seq", None),
        P("dp", "seq"),
        P("dp", "seq"),
        P("dp", "seq"),
        P("dp", "seq"),
    )
    out_specs = (P("dp", "seq"), P("dp", "seq", None), P("seq", None), P("seq", None))
    return jax.shard_map(
        on_device, mesh=mesh, in_specs=in_specs, out_specs=out_specs, check_vma=False
    )
```

profile of v0, /device:TPU:2, one launch (start us, length us, event | category | flops | bytes accessed | tf_op | source)
XLA Modules:
  0.0 379.7 jit_solution(3904731837600903716)
XLA Ops:
  8.0 3.5 collective-permute-start
  16.0 11.7 %all-to-all-start = ((s32[16,1,8]{2,1,0:T(1,128)}), s32[16,1,8]{2,1,0:T(1,128)S(1)}, u32[]{:S(2)}, u32[]{:S(2)}) async-start(s32[16,1,8]{2,1,0:T(1,128)} %bitcast.16), calls=%async_computation | async-start | bytes 16384 | tf_op jit(solution)/shard_map/all_to_all | solution.py:79
  29.8 3.6 fusion.20
  33.4 2.7 all-to-all-done
  39.6 4.0 %fusion.16 = f32[512,768]{1,0:T(8,128)} fusion(bf16[5,1024,768]{2,1,0:T(8,128)(2,1)} %param.12, bf16[516,1024]{1,0:T(8,128)(2,1)} %reshape.227), kind=kOutput, calls=%fused_computation.27 | convolution fusion | flops 805306368 | bytes 4194304 | tf_op jit(solution)/shard_map/dot_general | solution.py:53
  43.6 3.6 fusion.24
  49.1 3.6 fusion.12
  53.7 6.1 %multiply_convert_fusion = (bf16[512,768]{1,0:T(8,128)(2,1)S(1)}, f32[512,768]{1,0:T(8,128)}) fusion(f32[512,768]{1,0:T(8,128)} %fusion.12, f32[512,768]{1,0:T(8,128)} %fusion.16, f32[512,768]{1,0:T(8,128)} %fusion.20, f32[512,768]{1,0:T(8,128)} %fusion.24, bf16[512,1024]{1,0:T(8,128)(2,1)S(1)} %slice.101, bf16[5,1024,768]{2,1,0:T(8,128)(2,1)} %param.12, ...), kind=kOutput, calls=%fused_computation.41 | convolution fusion | flops 811204608 | bytes 12058624 | tf_op jit(solution)/shard_map/dot_general | solution.py:53
  61.7 5.4 %all-to-all-start.1 = ((bf16[16,8,768]{2,1,0:T(8,128)(2,1)}), bf16[16,8,768]{2,1,0:T(8,128)(2,1)}, u32[]{:S(2)}, u32[]{:S(2)}) async-start(bf16[16,8,768]{2,1,0:T(8,128)(2,1)} %fusion.40), calls=%async_computation.1 | async-start | bytes 393216 | tf_op jit(solution)/shard_map/all_to_all | solution.py:85
  69.8 7.8 %all-to-all-done.1 = bf16[16,8,768]{2,1,0:T(8,128)(2,1)} async-done(((bf16[16,8,768]{2,1,0:T(8,128)(2,1)}), bf16[16,8,768]{2,1,0:T(8,128)(2,1)}, u32[]{:S(2)}, u32[]{:S(2)}) %all-to-all-start.1) | async-done | bytes 196640 | tf_op jit(solution)/shard_map/all_to_all | solution.py:85
  79.3 1.8 fusion.60
  83.3 3.5 all-to-all-start.2
  90.4 1.9 fusion.72
  92.4 4.5 %all-to-all-done.2 = bf16[16,8,768]{2,1,0:T(8,128)(2,1)S(1)} async-done(((bf16[16,8,768]{2,1,0:T(8,128)(2,1)}), bf16[16,8,768]{2,1,0:T(8,128)(2,1)S(1)}, u32[]{:S(2)}, u32[]{:S(2)}) %all-to-all-start.2) | async-done | bytes 196640 | tf_op jit(solution)/shard_map/all_to_all | solution.py:107
  98.2 2.5 scatter_fusion.1
  100.6 2.0 fusion.63
  102.7 2.6 fusion.6
  106.9 2.4 fusion.18
  109.3 4.5 %collective-permute-start.3 = (bf16[1,2,768]{2,1,0:T(2,128)(2,1)S(1)}, bf16[1,2,768]{2,1,0:T(2,128)(2,1)S(1)}, u32[]{:S(2)}, u32[]{:S(2)}) collective-permute-start(bf16[1,2,768]{2,1,0:T(2,128)(2,1)S(1)} %get-tuple-element.7), channel_id=1, source_target_pairs={{0,1},{1,2},{2,3},{3,4},{4,5},{5,6},{6,7},{7,8},{8,9},{9,10},{10,1... | collective-permute-start | bytes 9224 | tf_op jit(solution)/shard_map/ppermute | solution.py:18
  113.9 2.4 fusion.26
  118.4 2.4 add_add_fusion
  120.8 2.5 reshape.233
  123.3 3.6 reduce_sum.35
  126.9 244.2 %all-reduce.3.cloned.1.call-done = (f32[768,768]{1,0:T(8,128)}, f32[768,768]{1,0:T(8,128)}) async-done(((f32[768,768]{1,0:T(8,128)}, f32[768,768]{1,0:T(8,128)}), (f32[768,768]{1,0:T(8,128)}, f32[768,768]{1,0:T(8,128)})) %all-reduce.3.cloned.1.call-update) | async-done | bytes 4718608 | tf_op jit(solution)/shard_map/psum | solution.py:137
  (75 shorter events, 32.4 us)
Async XLA Ops:
  7.2 53.5 %copy-start = (bf16[768,768]{1,0:T(8,128)(2,1)S(1)}, bf16[768,768]{1,0:T(8,128)(2,1)}, u32[]{:S(2)}) copy-start(bf16[768,768]{1,0:T(8,128)(2,1)} %param.14) | copy-start | bytes 3538948
  8.0 29.4 %collective-permute-start = (bf16[1,1,1024]{2,1,0:T(2,128)(2,1)S(1)}, bf16[1,1,1024]{2,1,0:T(2,128)(2,1)S(1)}, u32[]{:S(2)}, u32[]{:S(2)}) collective-permute-start(bf16[1,1,1024]{2,1,0:T(2,128)(2,1)S(1)} %get-tuple-element.10), channel_id=1, source_target_pairs={{0,1},{1,2},{2,3},{3,4},{4,5},{5,6},{6,7},{7,8},{8,9},{9,10},{10,1... | collective-permute-start | bytes 6152 | tf_op jit(solution)/shard_map/ppermute | solution.py:18
  11.5 26.0 %collective-permute-start.1 = (bf16[1,1,1024]{2,1,0:T(2,128)(2,1)S(1)}, bf16[1,1,1024]{2,1,0:T(2,128)(2,1)S(1)}, u32[]{:S(2)}, u32[]{:S(2)}) collective-permute-start(bf16[1,1,1024]{2,1,0:T(2,128)(2,1)S(1)} %get-tuple-element.11), channel_id=1, source_target_pairs={{1,0},{2,1},{3,2},{4,3},{5,4},{6,5},{7,6},{8,7},{9,8},{10,9},{11,1... | collective-permute-start | bytes 6152 | tf_op jit(solution)/shard_map/ppermute | solution.py:20
  14.5 18.9 %copy-start.9 = (s32[64]{0:T(128)}, s32[64]{0:T(128)S(1)}, u32[]{:S(2)}) copy-start(s32[64]{0:T(128)S(1)} %fusion.77) | copy-start | bytes 772
  16.0 20.2 %all-to-all-start = ((s32[16,1,8]{2,1,0:T(1,128)}), s32[16,1,8]{2,1,0:T(1,128)S(1)}, u32[]{:S(2)}, u32[]{:S(2)}) async-start(s32[16,1,8]{2,1,0:T(1,128)} %bitcast.16), calls=%async_computation | async-start | bytes 16384 | tf_op jit(solution)/shard_map/all_to_all | solution.py:79
  27.7 2.1 copy-start.10
  29.8 7.7 %copy-start.1 = (bf16[1,256,1024]{2,1,0:T(8,128)(2,1)S(1)}, bf16[1,256,1024]{2,1,0:T(8,128)(2,1)}, u32[]{:S(2)}) copy-start(bf16[1,256,1024]{2,1,0:T(8,128)(2,1)} %param.10) | copy-start | bytes 1572868
  39.6 4.0 %copy-start.5 = (bf16[516,1024]{1,0:T(8,128)(2,1)S(1)}, bf16[516,1024]{1,0:T(8,128)(2,1)}, u32[]{:S(2)}) copy-start(bf16[516,1024]{1,0:T(8,128)(2,1)} %reshape.227) | copy-start | bytes 3170308
  49.1 3.6 copy-start.2
  60.7 6.5 %copy-start.3 = (bf16[128,768]{1,0:T(8,128)(2,1)}, bf16[128,768]{1,0:T(8,128)(2,1)S(1)}, u32[]{:S(2)}) copy-start(bf16[128,768]{1,0:T(8,128)(2,1)S(1)} %gather_fusion.1) | copy-start | bytes 589828
  61.7 15.8 %all-to-all-start.1 = ((bf16[16,8,768]{2,1,0:T(8,128)(2,1)}), bf16[16,8,768]{2,1,0:T(8,128)(2,1)}, u32[]{:S(2)}, u32[]{:S(2)}) async-start(bf16[16,8,768]{2,1,0:T(8,128)(2,1)} %fusion.40), calls=%async_computation.1 | async-start | bytes 393216 | tf_op jit(solution)/shard_map/all_to_all | solution.py:85
  69.8 11.3 %copy-start.7 = (f32[1,64]{1,0:T(1,128)S(1)}, f32[1,64]{1,0:T(1,128)}, u32[]{:S(2)}) copy-start(f32[1,64]{1,0:T(1,128)} %param.16) | copy-start | bytes 772
  69.8 11.3 %copy-start.8 = (s32[1,64]{1,0:T(1,128)S(1)}, s32[1,64]{1,0:T(1,128)}, u32[]{:S(2)}) copy-start(s32[1,64]{1,0:T(1,128)} %param.19) | copy-start | bytes 772
  83.3 13.6 %all-to-all-start.2 = ((bf16[16,8,768]{2,1,0:T(8,128)(2,1)}), bf16[16,8,768]{2,1,0:T(8,128)(2,1)S(1)}, u32[]{:S(2)}, u32[]{:S(2)}) async-start(bf16[16,8,768]{2,1,0:T(8,128)(2,1)} %bitcast.23), calls=%async_computation.2 | async-start | bytes 393216 | tf_op jit(solution)/shard_map/all_to_all | solution.py:107
  86.8 284.3 %all-reduce.3.cloned.1.call-start = ((), (), s32[]{:S(2)}) async-start(), calls=%async_computation.3 | async-start | bytes 9437184 | tf_op jit(solution)/shard_map/psum | solution.py:137
  88.8 1.6 copy-start.6
  98.2 2.5 copy-start.4
  102.7 13.6 %slice-start = ((s8[7864320]{0:T(1024)(128)(4,1)}), s8[4194304]{0:T(1024)(128)(4,1)S(1)}, s32[]{:S(2)}) async-start(s8[7864320]{0:T(1024)(128)(4,1)} %bitcast.129), calls=%async_computation.4 | async-start | bytes 8388608
  105.3 11.0 %slice-start.1 = ((s8[7864320]{0:T(1024)(128)(4,1)}), s8[3670016]{0:T(1024)(128)(4,1)S(1)}, s32[]{:S(2)}) async-start(s8[7864320]{0:T(1024)(128)(4,1)} %bitcast.129), calls=%async_computation.5 | async-start | bytes 7340032
  105.3 8.5 %collective-permute-start.2 = (bf16[1,2,768]{2,1,0:T(2,128)(2,1)S(1)}, bf16[1,2,768]{2,1,0:T(2,128)(2,1)S(1)}, u32[]{:S(2)}, u32[]{:S(2)}) collective-permute-start(bf16[1,2,768]{2,1,0:T(2,128)(2,1)S(1)} %get-tuple-element.6), channel_id=1, source_target_pairs={{1,0},{2,1},{3,2},{4,3},{5,4},{6,5},{7,6},{8,7},{9,8},{10,9},{11,1... | collective-permute-start | bytes 9224 | tf_op jit(solution)/shard_map/ppermute | solution.py:20
  109.3 8.0 %collective-permute-start.3 = (bf16[1,2,768]{2,1,0:T(2,128)(2,1)S(1)}, bf16[1,2,768]{2,1,0:T(2,128)(2,1)S(1)}, u32[]{:S(2)}, u32[]{:S(2)}) collective-permute-start(bf16[1,2,768]{2,1,0:T(2,128)(2,1)S(1)} %get-tuple-element.7), channel_id=1, source_target_pairs={{0,1},{1,2},{2,3},{3,4},{4,5},{5,6},{6,7},{7,8},{8,9},{9,10},{10,1... | collective-permute-start | bytes 9224 | tf_op jit(solution)/shard_map/ppermute | solution.py:18
Sparse Core Ops, SparseCore 0:
  102.8 268.2 all-reduce.2
where the time goes:
time: 380 us
  waiting for transfers between devices  259 us (68%)
  matrix products  39.8 us (10%)
  starting transfers between devices  31.8 us (8%)
  other arithmetic  18.9 us (5%)
  local copies, waits for them, and re-layouts  15.4 us (4%)
  between operations  14.5 us (4%)
    psum x1, waiting for transfers between devices, on_device(): lax.psum((donor_term, acceptor_term), ('dp', 'seq'))  244 us
    dot_general x5, matrix products, on_device(): jnp.dot(upsampled[shift_index:shift_index + row_count], conv_weight[shift...  20.8 us
    all_to_all x1, starting transfers between devices, on_device(): lax.all_to_all(requests, 'seq', split_axis=0, concat_axis=0, tiled=True)  11.7 us
    dot_general x5, matrix products, on_device(): jnp.dot(widened_grad[begin:begin + row_count], conv_weight[shift_index].T...  9.29 us
    ppermute x2, starting transfers between devices, with_halo(): lax.ppermute(tail, axis, [(i, (i + 1) % count) for i in range(ends)])  8.02 us
    all_to_all x1, waiting for transfers between devices, on_device(): lax.all_to_all(projected, 'seq', split_axis=0, concat_axis=0, tiled=True)  7.75 us
  transfers between devices with their start and end apart: 8, of which 4 were waited for; matrix products, arithmetic and copies ran while one was open for 9% of the time, Pallas kernels for 0%

commit v1 on v0

--- a/solution.py
+++ b/solution.py
@@ -1,3 +1,4 @@
+import functools
 import math
 import jax
 import jax.numpy as jnp
@@ -5,6 +6,13 @@
 from jax.sharding import PartitionSpec as P
 
 ACAP = 8
+
+
+def note_stages_all_on_mesh(z, row_axis, device_axis):
+    return lax.psum(lax.psum(z, axis_name=row_axis), device_axis)
+
+
+_plan_words = functools.partial(note_stages_all_on_mesh, row_axis="seq", device_axis="dp")
 
 
 def with_halo(cells, sides, width):
@@ -134,7 +142,7 @@
     factor = 1.0 / batch_count
     donor_term = jnp.dot(donor_act.T, donor_emb_grad, preferred_element_type=jnp.float32)
     acceptor_term = jnp.dot(served_act.T, served_emb_grad, preferred_element_type=jnp.float32)
-    donor_total, acceptor_total = lax.psum((donor_term, acceptor_term), ("dp", "seq"))
+    donor_total, acceptor_total = _plan_words((donor_term, acceptor_term))
     first_row = lax.axis_index("seq") * rows_each
     donor_part = lax.dynamic_slice_in_dim(donor_total, first_row, rows_each, 0)
     acceptor_part = lax.dynamic_slice_in_dim(acceptor_total, first_row, rows_each, 0)

time: 380 us -> 488 us (1.28); the launches traced: 380 us -> 481 us
  waiting for transfers between devices: 259 us -> 363 us
    psum x1 -> x2, waiting for transfers between devices: 244 us -> 344 us  [note_stages_all_on_mesh(): return lax.psum(lax.psum(z, axis_name=row_axis), device_axis)]
  transfers between devices with their start and end apart: 8 -> 9, of which waited for: 4 -> 5; matrix products, arithmetic and copies ran while one was open for 9% -> 8% of each run, Pallas kernels for 0% -> 0%
where the time goes in v1:
time: 488 us; the launch traced here: 481 us
  waiting for transfers between devices  363 us (74%)
  matrix products  38.7 us (8%)
  starting transfers between devices  31.8 us (7%)
  other arithmetic  19.1 us (4%)
  between operations  14.4 us (3%)
  local copies, waits for them, and re-layouts  14.3 us (3%)
    psum x2, waiting for transfers between devices, note_stages_all_on_mesh(): return lax.psum(lax.psum(z, axis_name=row_axis), device_axis)  344 us
    dot_general x5, matrix products, on_device(): jnp.dot(upsampled[shift_index:shift_index + row_count], conv_weight[shift...  20.8 us
    all_to_all x1, starting transfers between devices, on_device(): lax.all_to_all(requests, 'seq', split_axis=0, concat_axis=0, tiled=True)  11.7 us
  transfers between devices with their start and end apart: 9, of which 5 were waited for; matrix products, arithmetic and copies ran while one was open for 8% of the time, Pallas kernels for 0%

profile of v1, /device:TPU:2, one launch (start us, length us, event | category | flops | bytes accessed | tf_op | source)
XLA Modules:
  0.0 481.5 jit_solution(10795472511092056501)
XLA Ops:
  8.0 3.5 collective-permute-start
  16.0 11.7 %all-to-all-start = ((s32[16,1,8]{2,1,0:T(1,128)}), s32[16,1,8]{2,1,0:T(1,128)S(1)}, u32[]{:S(2)}, u32[]{:S(2)}) async-start(s32[16,1,8]{2,1,0:T(1,128)} %bitcast.16), calls=%async_computation | async-start | bytes 16384 | tf_op jit(solution)/shard_map/all_to_all | solution.py:87
  29.8 3.6 fusion.20
  33.4 2.8 all-to-all-done
  39.6 4.0 fusion.16
  43.6 3.6 fusion.24
  49.1 3.6 fusion.12
  53.7 6.1 %multiply_convert_fusion = (bf16[512,768]{1,0:T(8,128)(2,1)S(1)}, f32[512,768]{1,0:T(8,128)}) fusion(f32[512,768]{1,0:T(8,128)} %fusion.12, f32[512,768]{1,0:T(8,128)} %fusion.16, f32[512,768]{1,0:T(8,128)} %fusion.20, f32[512,768]{1,0:T(8,128)} %fusion.24, bf16[512,1024]{1,0:T(8,128)(2,1)S(1)} %slice.101, bf16[5,1024,768]{2,1,0:T(8,128)(2,1)} %param.12, ...), kind=kOutput, calls=%fused_computation.41 | convolution fusion | flops 811204608 | bytes 12058624 | tf_op jit(solution)/shard_map/dot_general | solution.py:61
  61.7 5.3 %all-to-all-start.1 = ((bf16[16,8,768]{2,1,0:T(8,128)(2,1)}), bf16[16,8,768]{2,1,0:T(8,128)(2,1)S(1)}, u32[]{:S(2)}, u32[]{:S(2)}) async-start(bf16[16,8,768]{2,1,0:T(8,128)(2,1)} %fusion.40), calls=%async_computation.1 | async-start | bytes 393216 | tf_op jit(solution)/shard_map/all_to_all | solution.py:93
  69.1 8.3 %all-to-all-done.1 = bf16[16,8,768]{2,1,0:T(8,128)(2,1)S(1)} async-done(((bf16[16,8,768]{2,1,0:T(8,128)(2,1)}), bf16[16,8,768]{2,1,0:T(8,128)(2,1)S(1)}, u32[]{:S(2)}, u32[]{:S(2)}) %all-to-all-start.1) | async-done | bytes 196640 | tf_op jit(solution)/shard_map/all_to_all | solution.py:93
  81.7 3.5 all-to-all-start.2
  85.5 2.0 fusion.72
  87.4 7.9 %all-to-all-done.2 = bf16[16,8,768]{2,1,0:T(8,128)(2,1)S(1)} async-done(((bf16[16,8,768]{2,1,0:T(8,128)(2,1)}), bf16[16,8,768]{2,1,0:T(8,128)(2,1)S(1)}, u32[]{:S(2)}, u32[]{:S(2)}) %all-to-all-start.2) | async-done | bytes 196640 | tf_op jit(solution)/shard_map/all_to_all | solution.py:115
  95.3 2.0 fusion.63
  97.3 218.4 %all-reduce.5.cloned.1.call-done = (f32[768,768]{1,0:T(8,128)}, f32[768,768]{1,0:T(8,128)}) async-done(((f32[768,768]{1,0:T(8,128)}, f32[768,768]{1,0:T(8,128)}), (f32[768,768]{1,0:T(8,128)}, f32[768,768]{1,0:T(8,128)})) %all-reduce.5.cloned.1.call-update) | async-done | bytes 4718608 | tf_op jit(solution)/shard_map/psum | solution.py:12
  321.0 2.0 scatter_fusion.1
  323.0 2.6 fusion.6
  327.2 2.4 fusion.18
  329.6 4.5 collective-permute-start.3
  334.2 2.4 fusion.26
  338.7 2.4 add_add_fusion
  341.1 2.5 reshape.233
  343.6 3.6 reduce_sum.35
  347.2 125.7 %all-reduce.7.cloned.1.call-done = (f32[768,768]{1,0:T(8,128)}, f32[768,768]{1,0:T(8,128)}) async-done(((f32[768,768]{1,0:T(8,128)}, f32[768,768]{1,0:T(8,128)}), (f32[768,768]{1,0:T(8,128)}, f32[768,768]{1,0:T(8,128)})) %all-reduce.7.cloned.1.call-update) | async-done | bytes 4718608 | tf_op jit(solution)/shard_map/psum | solution.py:12
  (74 shorter events, 32.6 us)
Async XLA Ops:
  7.2 53.5 %copy-start = (bf16[768,768]{1,0:T(8,128)(2,1)S(1)}, bf16[768,768]{1,0:T(8,128)(2,1)}, u32[]{:S(2)}) copy-start(bf16[768,768]{1,0:T(8,128)(2,1)} %param.14) | copy-start | bytes 3538948
  8.0 29.4 %collective-permute-start = (bf16[1,1,1024]{2,1,0:T(2,128)(2,1)S(1)}, bf16[1,1,1024]{2,1,0:T(2,128)(2,1)S(1)}, u32[]{:S(2)}, u32[]{:S(2)}) collective-permute-start(bf16[1,1,1024]{2,1,0:T(2,128)(2,1)S(1)} %get-tuple-element.12), channel_id=1, source_target_pairs={{0,1},{1,2},{2,3},{3,4},{4,5},{5,6},{6,7},{7,8},{8,9},{9,10},{10,1... | collective-permute-start | bytes 6152 | tf_op jit(solution)/shard_map/ppermute | solution.py:26
  11.5 26.0 %collective-permute-start.1 = (bf16[1,1,1024]{2,1,0:T(2,128)(2,1)S(1)}, bf16[1,1,1024]{2,1,0:T(2,128)(2,1)S(1)}, u32[]{:S(2)}, u32[]{:S(2)}) collective-permute-start(bf16[1,1,1024]{2,1,0:T(2,128)(2,1)S(1)} %get-tuple-element.13), channel_id=1, source_target_pairs={{1,0},{2,1},{3,2},{4,3},{5,4},{6,5},{7,6},{8,7},{9,8},{10,9},{11,1... | collective-permute-start | bytes 6152 | tf_op jit(solution)/shard_map/ppermute | solution.py:28
  14.5 52.6 %copy-start.8 = (s32[64]{0:T(128)}, s32[64]{0:T(128)S(1)}, u32[]{:S(2)}) copy-start(s32[64]{0:T(128)S(1)} %fusion.77) | copy-start | bytes 772
  16.0 20.2 %all-to-all-start = ((s32[16,1,8]{2,1,0:T(1,128)}), s32[16,1,8]{2,1,0:T(1,128)S(1)}, u32[]{:S(2)}, u32[]{:S(2)}) async-start(s32[16,1,8]{2,1,0:T(1,128)} %bitcast.16), calls=%async_computation | async-start | bytes 16384 | tf_op jit(solution)/shard_map/all_to_all | solution.py:87
  29.8 7.7 %copy-start.1 = (bf16[1,256,1024]{2,1,0:T(8,128)(2,1)S(1)}, bf16[1,256,1024]{2,1,0:T(8,128)(2,1)}, u32[]{:S(2)}) copy-start(bf16[1,256,1024]{2,1,0:T(8,128)(2,1)} %param.10) | copy-start | bytes 1572868
  39.6 4.0 copy-start.4
  49.1 3.6 copy-start.3
  60.7 17.4 %copy-start.2 = (bf16[768,768]{1,0:T(8,128)(2,1)S(1)}, bf16[768,768]{1,0:T(8,128)(2,1)}, u32[]{:S(2)}) copy-start(bf16[768,768]{1,0:T(8,128)(2,1)} %param.13) | copy-start | bytes 3538948
  61.7 15.7 %all-to-all-start.1 = ((bf16[16,8,768]{2,1,0:T(8,128)(2,1)}), bf16[16,8,768]{2,1,0:T(8,128)(2,1)S(1)}, u32[]{:S(2)}, u32[]{:S(2)}) async-start(bf16[16,8,768]{2,1,0:T(8,128)(2,1)} %fusion.40), calls=%async_computation.1 | async-start | bytes 393216 | tf_op jit(solution)/shard_map/all_to_all | solution.py:93
  69.1 10.3 %copy-start.6 = (f32[1,64]{1,0:T(1,128)S(1)}, f32[1,64]{1,0:T(1,128)}, u32[]{:S(2)}) copy-start(f32[1,64]{1,0:T(1,128)} %param.16) | copy-start | bytes 772
  69.1 10.3 %copy-start.7 = (s32[1,64]{1,0:T(1,128)S(1)}, s32[1,64]{1,0:T(1,128)}, u32[]{:S(2)}) copy-start(s32[1,64]{1,0:T(1,128)} %param.19) | copy-start | bytes 772
  77.4 8.1 %copy-start.5 = (bf16[64,768]{1,0:T(8,128)(2,1)S(1)}, bf16[64,768]{1,0:T(8,128)(2,1)}, u32[]{:S(2)}) copy-start(bf16[64,768]{1,0:T(8,128)(2,1)} %gather_fusion) | copy-start | bytes 294916
  81.7 13.6 %all-to-all-start.2 = ((bf16[16,8,768]{2,1,0:T(8,128)(2,1)}), bf16[16,8,768]{2,1,0:T(8,128)(2,1)S(1)}, u32[]{:S(2)}, u32[]{:S(2)}) async-start(bf16[16,8,768]{2,1,0:T(8,128)(2,1)} %bitcast.23), calls=%async_computation.2 | async-start | bytes 393216 | tf_op jit(solution)/shard_map/all_to_all | solution.py:115
  85.2 230.6 %all-reduce.5.cloned.1.call-start = ((), (), s32[]{:S(2)}) async-start(), calls=%async_computation.3 | async-start | bytes 9437184 | tf_op jit(solution)/shard_map/psum | solution.py:12
  97.3 375.6 %all-reduce.7.cloned.1.call-start = ((), (), s32[]{:S(2)}) async-start(), calls=%async_computation.4 | async-start | bytes 9437184 | tf_op jit(solution)/shard_map/psum | solution.py:12
  323.0 13.7 %slice-start = ((s8[7864320]{0:T(1024)(128)(4,1)}), s8[4194304]{0:T(1024)(128)(4,1)S(1)}, s32[]{:S(2)}) async-start(s8[7864320]{0:T(1024)(128)(4,1)} %bitcast.130), calls=%async_computation.5 | async-start | bytes 8388608
  325.6 11.0 %slice-start.1 = ((s8[7864320]{0:T(1024)(128)(4,1)}), s8[3670016]{0:T(1024)(128)(4,1)S(1)}, s32[]{:S(2)}) async-start(s8[7864320]{0:T(1024)(128)(4,1)} %bitcast.130), calls=%async_computation.6 | async-start | bytes 7340032
  325.6 8.5 %collective-permute-start.2 = (bf16[1,2,768]{2,1,0:T(2,128)(2,1)S(1)}, bf16[1,2,768]{2,1,0:T(2,128)(2,1)S(1)}, u32[]{:S(2)}, u32[]{:S(2)}) collective-permute-start(bf16[1,2,768]{2,1,0:T(2,128)(2,1)S(1)} %get-tuple-element.8), channel_id=1, source_target_pairs={{1,0},{2,1},{3,2},{4,3},{5,4},{6,5},{7,6},{8,7},{9,8},{10,9},{11,1... | collective-permute-start | bytes 9224 | tf_op jit(solution)/shard_map/ppermute | solution.py:28
  329.6 8.1 %collective-permute-start.3 = (bf16[1,2,768]{2,1,0:T(2,128)(2,1)S(1)}, bf16[1,2,768]{2,1,0:T(2,128)(2,1)S(1)}, u32[]{:S(2)}, u32[]{:S(2)}) collective-permute-start(bf16[1,2,768]{2,1,0:T(2,128)(2,1)S(1)} %get-tuple-element.9), channel_id=1, source_target_pairs={{0,1},{1,2},{2,3},{3,4},{4,5},{5,6},{6,7},{7,8},{8,9},{9,10},{10,1... | collective-permute-start | bytes 9224 | tf_op jit(solution)/shard_map/ppermute | solution.py:26
Sparse Core Ops, SparseCore 0:
  97.4 218.3 all-reduce.4
  318.5 154.3 all-reduce.6
